TPU v7x, 512 devices: a whole 4x4x16 slice. The times are simulated.
512 devices in a mesh: ctx: 64 (over x, z), head: 8 (over y, core).
Axes of the slice: x: 4, y: 4, z: 16, core: 2. Of those that a mesh axis runs over, the one named last changes fastest.
Arguments:
- lin_queries: bfloat16 [8192, 4096], P('ctx', 'head'), may hold values from -6 to 6
- lin_keys: bfloat16 [8192, 4096], P('ctx', 'head'), may hold values from -6 to 6
- lin_values: bfloat16 [8192, 4096], P('ctx', 'head'), may hold values from -6 to 6
- state_in: float32 [32, 128, 128], P('head'), may hold values from -24 to 24
- decay_exps: int32 [32], P('head'), may hold values from 5 to 13
- soft_queries: bfloat16 [8192, 4096], P('ctx', 'head'), may hold values from -80 to 80
- soft_keys: bfloat16 [8192, 1024], P('ctx', 'head'), may hold values from -4 to 4
- soft_values: bfloat16 [8192, 1024], P('ctx', 'head'), may hold values from -6 to 6
- lin_gain: float32 [4096], P('head'), may hold values from 0.5 to 1.5
- soft_gain: float32 [4096], P('head'), may hold values from 0.5 to 1.5
- lin_weight: bfloat16 [4096, 3072], P(('head', 'ctx')), may hold values from -0.09375 to 0.09375
- soft_weight: bfloat16 [4096, 3072], P(('head', 'ctx')), may hold values from -0.09375 to 0.09375
Outputs:
- lin_projected: bfloat16 [8192, 3072], P('ctx', 'head')
- soft_projected: bfloat16 [8192, 3072], P('ctx', 'head')
All inputs are finite; a program needn't handle non-finite values.
Results may differ from a plain program's by a relative error of at most 0.019.
Values may be sent and summed in bfloat16 or wider, within the bound.
A program may use at most 128 MiB of HBM per device.

v0:
```python
import jax
import jax.numpy as jnp
from jax import lax
from jax.sharding import PartitionSpec as P

HEADS = 32
KV_HEADS = 8
HEAD_DIM = 128


HIGH = lax.Precision.HIGHEST


def carried_in(part, axis, combine, identity):
    place = lax.axis_index(axis)
    gathered = jax.tree.map(lambda a: lax.all_gather(a, axis), part)
    state = jax.tree.map(lambda a, e: jnp.zeros_like(a) + jnp.asarray(e, a.dtype), part, identity)

    def one(turn, state):
        return combine(
            state, jax.tree.map(lambda a: lax.dynamic_index_in_dim(a, turn, 0, False), gathered)
        )

    return lax.fori_loop(0, place, one, state)


def branch_norm(values, gain):
    scale = lax.rsqrt(jnp.mean(values * values, axis=-1, keepdims=True) + 1e-06)
    return values * scale * gain.reshape(values.shape[-2], values.shape[-1])


def chain_combine(earlier, later):
    return (earlier[0] * later[0], later[0][:, None, None] * earlier[1] + later[1])


def local(
    lin_queries,
    lin_keys,
    lin_values,
    state_in,
    decay_exps,
    soft_queries,
    soft_keys,
    soft_values,
    lin_gain,
    soft_gain,
    lin_weight,
    soft_weight,
):
    block = lin_queries.shape[0]
    local_heads = lin_queries.shape[1] // HEAD_DIM
    local_kv = soft_keys.shape[1] // HEAD_DIM
    group = HEADS // KV_HEADS
    factor = 1.0 / HEAD_DIM**0.5
    rates = jnp.exp2(-decay_exps.astype(jnp.float32))
    offsets = jnp.arange(block).astype(jnp.float32)
    within = offsets[:, None] - offsets[None, :]
    inside = jnp.where(
        (within >= 0)[None], jnp.exp(-rates[:, None, None] * jnp.maximum(within, 0.0)[None]), 0.0
    )
    query_decay = jnp.exp(-rates[None, :] * (offsets[:, None] + 1.0))
    key_decay = jnp.exp(-rates[None, :] * (block - 1.0 - offsets[:, None]))
    block_decay = jnp.exp(-rates * block)
    queries = lin_queries.astype(jnp.float32).reshape(block, local_heads, HEAD_DIM)
    keys = lin_keys.astype(jnp.float32).reshape(block, local_heads, HEAD_DIM)
    values = lin_values.astype(jnp.float32).reshape(block, local_heads, HEAD_DIM)
    update = jnp.einsum("uhd,uhe->hde", keys * key_decay[:, :, None], values, precision=HIGH)
    identity = (
        jnp.ones((local_heads,), jnp.float32),
        jnp.zeros((local_heads, HEAD_DIM, HEAD_DIM), jnp.float32),
    )
    decay_before, carried = carried_in((block_decay, update), "ctx", chain_combine, identity)
    scores = jnp.einsum("thd,uhd->htu", queries, keys, precision=HIGH) * inside
    intra = jnp.einsum("htu,uhd->thd", scores, values, precision=HIGH)
    entering = decay_before[:, None, None] * state_in + carried
    inter = jnp.einsum("thd,hde->the", queries * query_decay[:, :, None], entering, precision=HIGH)
    lin_norm = (
        branch_norm(intra + inter, lin_gain)
        .reshape(block, local_heads * HEAD_DIM)
        .astype(jnp.bfloat16)
    )
    soft_local = soft_queries.reshape(block, local_kv, group, HEAD_DIM)
    query_positions = lax.axis_index("ctx") * block + jnp.arange(block)
    piece = (
        lax.all_gather(soft_keys, "ctx", axis=0, tiled=True),
        lax.all_gather(soft_values, "ctx", axis=0, tiled=True),
    )
    peak = jnp.full((block, local_kv, group), -1e30, jnp.float32)
    piece_keys = piece[0].reshape(piece[0].shape[0], local_kv, HEAD_DIM)
    piece_values = piece[1].reshape(piece[1].shape[0], local_kv, HEAD_DIM)
    raw = (
        jnp.einsum("tcgd,ucd->tcgu", soft_local, piece_keys, preferred_element_type=jnp.float32)
        * factor
    )
    key_positions = jnp.arange(piece_keys.shape[0])
    causal = (key_positions[None, :] <= query_positions[:, None])[:, None, None, :]
    raw = jnp.where(causal, raw, -1e30)
    new_peak = jnp.maximum(peak, jnp.max(raw, axis=-1))
    weights = jnp.where(causal, jnp.exp(raw - new_peak[..., None]), 0.0)
    summed = jnp.sum(weights, axis=-1)
    product = jnp.einsum(
        "tcgu,ucd->tcgd",
        weights.astype(jnp.bfloat16),
        piece_values,
        preferred_element_type=jnp.float32,
    )
    soft_out = (product / summed[..., None]).reshape(block, local_heads, HEAD_DIM)
    soft_norm = (
        branch_norm(soft_out, soft_gain).reshape(block, local_heads * HEAD_DIM).astype(jnp.bfloat16)
    )
    piece = (
        lax.all_gather(lin_weight, "ctx", axis=0, tiled=True),
        lax.all_gather(soft_weight, "ctx", axis=0, tiled=True),
    )
    lin_partial = jnp.dot(lin_norm, piece[0], preferred_element_type=jnp.float32)
    soft_partial = jnp.dot(soft_norm, piece[1], preferred_element_type=jnp.float32)
    lin_sum, soft_sum = (
        lax.psum_scatter(
            lin_partial.astype(jnp.bfloat16), "head", scatter_dimension=1, tiled=True
        ).astype(jnp.float32),
        lax.psum_scatter(
            soft_partial.astype(jnp.bfloat16), "head", scatter_dimension=1, tiled=True
        ).astype(jnp.float32),
    )
    return (lin_sum.astype(jnp.bfloat16), soft_sum.astype(jnp.bfloat16))


def solution(mesh):
    placed = (
        P("ctx", "head"),
        P("ctx", "head"),
        P("ctx", "head"),
        P("head", None, None),
        P("head"),
        P("ctx", "head"),
        P("ctx", "head"),
        P("ctx", "head"),
        P("head"),
        P("head"),
        P(("head", "ctx"), None),
        P(("head", "ctx"), None),
    )
    return jax.shard_map(
        local,
        mesh=mesh,
        in_specs=placed,
        out_specs=(P("ctx", "head"), P("ctx", "head")),
        check_vma=False,
    )
```

profile of v0, /device:TPU:1, one launch (start us, length us, event | category | flops | bytes accessed | tf_op | source)
XLA Modules:
  0.0 853.4 jit_solution(13072365497063753452)
XLA Ops:
  7.2 0.0 copy-start
  7.2 0.0 all-gather.10.cloned.1.call-start
  7.2 0.7 all-gather.10.cloned.1.call-update
  7.9 0.0 all-gather.12.cloned.1.call-start
  8.0 1.5 copy.38
  9.4 0.0 all-gather.12.cloned.1.call-update
  9.5 0.0 all-gather.14.cloned.1.call-start
  9.5 0.7 all-gather.14.cloned.1.call-update
  10.2 0.0 all-gather.16.cloned.1.call-start
  10.3 1.0 copy.46
  11.3 1.3 dynamic-slice
  13.2 0.8 exponential_dynamic-update-slice_fusion
  14.0 0.1 multiply_exponential_fusion
  14.1 1.9 fusion.28
  15.9 0.0 all-gather.16.cloned.1.call-update
  16.0 0.0 all-gather.8.cloned.1.call-start
  16.0 0.5 all-gather.8.cloned.1.call-update
  16.6 0.0 reduce-scatter.9.cloned.1.call-start
  16.6 0.1 subtract_maximum_fusion
  16.7 0.1 subtract_compare_fusion
  16.8 122.8 %all-reduce = f32[256]{0:T(256)S(1)} all-reduce(f32[256]{0:T(256)S(1)} %get-tuple-element.54), channel_id=2, replica_groups=mesh['ctx'=64,'head'=8] {'ctx'}, use_global_device_ids=true, to_apply=%add | all-reduce | flops 256 | bytes 2048
  139.6 0.1 reshape.240
  139.7 1.1 convolution_multiply_fusion
  140.8 1.3 convolution_bitcast_fusion.1
  142.2 0.7 iota_compare_fusion
  142.9 5.6 all-gather.10.cloned.1.call-done
  148.5 0.0 copy-done
  148.5 3.8 fusion
  152.3 0.0 copy-start.1
  152.3 5.7 copy-done.1
  158.0 4.1 fusion.1
  162.2 0.0 copy-start.4
  162.2 0.0 copy-start.2
  162.2 0.0 copy-start.3
  162.2 0.0 copy-start.5
  162.2 120.6 %all-gather.12.cloned.1.call-done = bf16[8192,128]{0,1:T(8,128)(2,1)} async-done(((bf16[128,128]{0,1:T(8,128)(2,1)}), bf16[8192,128]{0,1:T(8,128)(2,1)}) %all-gather.12.cloned.1.call-update) | async-done | bytes 2097168 | tf_op jit(solution)/shard_map/all_gather | solution.py:86
  282.8 8.5 fusion.23
  291.2 0.0 copy-done.4
  291.2 0.1 fusion.22
  291.4 135.7 %all-gather.14.cloned.1.call-done = bf16[512,3072]{1,0:T(8,128)(2,1)} async-done(((bf16[8,3072]{1,0:T(8,128)(2,1)}), bf16[512,3072]{1,0:T(8,128)(2,1)}) %all-gather.14.cloned.1.call-update) | async-done | bytes 3145744 | tf_op jit(solution)/shard_map/all_gather | solution.py:113
  427.1 2.5 convolution_convert_fusion
  429.6 1.2 copy.44
  430.8 0.0 reduce-scatter.9.cloned.1.call-update
  430.8 0.0 reduce-scatter.7.cloned.1.call-start
  430.9 194.8 %all-gather.16.cloned.1.call-done = f32[256,128,128]{2,1,0:T(8,128)} async-done(((f32[4,128,128]{2,1,0:T(8,128)}), f32[256,128,128]{2,1,0:T(8,128)}) %all-gather.16.cloned.1.call-update) | async-done | bytes 16777232 | tf_op jit(solution)/shard_map/all_gather | solution.py:16
  625.7 0.0 copy-done.2
  625.7 0.0 copy-done.3
  625.8 0.7 multiply_reduce_fusion
  626.5 0.0 copy-done.5
  626.5 0.1 multiply_convert_fusion
  626.6 134.5 %all-gather.8.cloned.1.call-done = bf16[512,3072]{1,0:T(8,128)(2,1)} async-done(((bf16[8,3072]{1,0:T(8,128)(2,1)}), bf16[512,3072]{1,0:T(8,128)(2,1)}) %all-gather.8.cloned.1.call-update) | async-done | bytes 3145744 | tf_op jit(solution)/shard_map/all_gather | solution.py:112
  761.2 2.5 convolution_convert_fusion.1
  763.6 1.2 copy.42
  764.8 0.0 reduce-scatter.7.cloned.1.call-update
  764.9 38.9 %reduce-scatter.9.cloned.1.call-done = bf16[384,128]{1,0:T(8,128)(2,1)} async-done(((bf16[3072,128]{1,0:T(8,128)(2,1)}), bf16[384,128]{1,0:T(8,128)(2,1)}) %reduce-scatter.9.cloned.1.call-update) | async-done | bytes 98320
  803.8 1.6 copy.45
  805.4 39.4 %reduce-scatter.7.cloned.1.call-done = bf16[384,128]{1,0:T(8,128)(2,1)} async-done(((bf16[3072,128]{1,0:T(8,128)(2,1)}), bf16[384,128]{1,0:T(8,128)(2,1)}) %reduce-scatter.7.cloned.1.call-update) | async-done | bytes 98320
  844.9 1.6 copy.43
  (10 shorter events, 0.1 us)
Async XLA Ops:
  7.2 141.3 %copy-start = (bf16[128,512]{1,0:T(8,128)(2,1)S(1)}, bf16[128,512]{1,0:T(8,128)(2,1)}, u32[]{:S(2)}) copy-start(bf16[128,512]{1,0:T(8,128)(2,1)} %param.19) | copy-start | bytes 393220
  7.2 141.3 %all-gather.10.cloned.1.call-start = ((), (), s32[]{:S(2)}) async-start(), calls=%async_computation.3 | async-start | bytes 2129920 | tf_op jit(solution)/shard_map/all_gather | solution.py:85
  7.9 274.8 %all-gather.12.cloned.1.call-start = ((), (), s32[]{:S(2)}) async-start(), calls=%async_computation.4 | async-start | bytes 2129920 | tf_op jit(solution)/shard_map/all_gather | solution.py:86
  9.5 417.6 %all-gather.14.cloned.1.call-start = ((), (), s32[]{:S(2)}) async-start(), calls=%async_computation.5 | async-start | bytes 3194880 | tf_op jit(solution)/shard_map/all_gather | solution.py:113
  10.2 615.5 %all-gather.16.cloned.1.call-start = ((), (), s32[]{:S(2)}) async-start(), calls=%async_computation.6 | async-start | bytes 17039360 | tf_op jit(solution)/shard_map/all_gather | solution.py:16
  16.0 745.2 %all-gather.8.cloned.1.call-start = ((), (), s32[]{:S(2)}) async-start(), calls=%async_computation.2 | async-start | bytes 3194880 | tf_op jit(solution)/shard_map/all_gather | solution.py:112
  16.6 787.2 %reduce-scatter.9.cloned.1.call-start = ((), (), s32[]{:S(2)}) async-start(), calls=%async_computation.8 | async-start | bytes 884736
  152.3 5.7 copy-start.1
  162.2 129.1 %copy-start.4 = (f32[512]{0:T(512)S(1)}, f32[512]{0:T(512)}, u32[]{:S(2)}) copy-start(f32[512]{0:T(512)} %param.23) | copy-start | bytes 6148
  162.2 463.6 %copy-start.2 = (bf16[128,512]{1,0:T(8,128)(2,1)S(1)}, bf16[128,512]{1,0:T(8,128)(2,1)}, u32[]{:S(2)}) copy-start(bf16[128,512]{1,0:T(8,128)(2,1)} %param.14) | copy-start | bytes 393220
  162.2 463.6 %copy-start.3 = (f32[4,128,128]{2,1,0:T(8,128)S(1)}, f32[4,128,128]{2,1,0:T(8,128)}, u32[]{:S(2)}) copy-start(f32[4,128,128]{2,1,0:T(8,128)} %param.17) | copy-start | bytes 786436
  162.2 464.3 %copy-start.5 = (f32[512]{0:T(512)S(1)}, f32[512]{0:T(512)}, u32[]{:S(2)}) copy-start(f32[512]{0:T(512)} %param.22) | copy-start | bytes 6148
  430.8 414.1 %reduce-scatter.7.cloned.1.call-start = ((), (), s32[]{:S(2)}) async-start(), calls=%async_computation.7 | async-start | bytes 884736
Sparse Core Ops, SparseCore 0:
  11.0 137.5 all-gather.9
  152.0 130.7 all-gather.11
  285.7 141.3 all-gather.13
  429.9 195.7 all-gather.15
  628.5 132.6 all-gather.7
  763.8 39.9 reduce-scatter.8
  806.9 37.9 reduce-scatter.6
where the time goes:
time: 857 us; the launch traced here: 853 us
  waiting for transfers between devices  672 us (78%)
  blocking collectives  123 us (14%)
  matrix products  22.2 us (3%)
  local copies, waits for them, and re-layouts  15.3 us (2%)
  between operations  15 us (2%)
    all_gather x1, waiting for transfers between devices, carried_in(): gathered = jax.tree.map(lambda a: lax.all_gather(a, axis), part)  195 us
    all_gather x1, waiting for transfers between devices, local(): lax.all_gather(soft_weight, 'ctx', axis=0, tiled=True)  136 us
    all_gather x1, waiting for transfers between devices, local(): lax.all_gather(lin_weight, 'ctx', axis=0, tiled=True)  135 us
    unnamed x1, blocking collectives  123 us
    all_gather x1, waiting for transfers between devices, local(): lax.all_gather(soft_values, 'ctx', axis=0, tiled=True)  121 us
    unnamed x9, waiting for transfers between devices  80.3 us
  transfers between devices with their start and end apart: 7, of which 7 were waited for; matrix products, arithmetic and copies ran while one was open for 4% of the time, Pallas kernels for 0%

commit v1 on v0

v1 whole, which is shorter than its diff:
```python
import functools

import jax
import jax.numpy as jnp
from jax import lax
from jax.experimental import pallas as pl
from jax.experimental.pallas import tpu as pltpu
from jax.sharding import PartitionSpec as P

D = 128
H = 4
TOK = 128
NOUT = 384
MESH = pl.DeviceIdType.MESH
BF = jnp.bfloat16
F32 = jnp.float32
NEG = -1e30
FLOOR = -1e29


def dot(a, b):
    return jnp.dot(a, b, preferred_element_type=F32)


def dot_t(a, b):
    return lax.dot_general(a, b, (((1,), (1,)), ((), ())), preferred_element_type=F32)


def split2(a):
    hi = a.astype(BF)
    return hi, (a - hi.astype(F32)).astype(BF)


def iota(shape, axis):
    return lax.broadcasted_iota(jnp.int32, shape, axis)


def head_norm(values, gain):
    scale = lax.rsqrt(jnp.mean(values * values, axis=-1, keepdims=True) + 1e-06)
    return values * scale * gain


def kernel(
    nx, nz, lq, lk, lv, st, de, sq, sk, sv, lg, sg, lw, sw, lo, so,
    kvst, kvg, qst, qh, wst, wland, wg, us, uland, tx, ss, sland,
    osend, oland, lsend, lland, ag, csend, cland, perm, bias,
    kvt_s, kvt_r, wt_s, wt_r, qt_s, qt_r, ua_s, ua_r, tx_s, tx_r, sa_s, sa_r,
    kv_s, kv_r, wr_s, wr_r, os_s, os_r, ls_s, ls_r, lat_s, lat_r, sat_s, sat_r,
    fw_s, fw_r, cs_s, cs_r,
):
    ny = nx
    half = nz // 2
    rows = lw.shape[0]
    sub = TOK // ny
    span = nz * sub
    depth = H * D
    part = depth // nz
    ctx, head = lax.axis_index("ctx"), lax.axis_index("head")
    x, z = ctx // nz, ctx % nz
    y, c = head // 2, head % 2

    def dev(dx, dy, dz, dc):
        return (dx * nz + dz, dy * 2 + dc)

    def remote(src, dst, ssem, rsem, to):
        return pltpu.make_async_remote_copy(
            src_ref=src, dst_ref=dst, send_sem=ssem, recv_sem=rsem, device_id=to, device_id_type=MESH
        )

    on_diag = x == y

    barrier = pltpu.get_barrier_semaphore()

    def greet(to):
        pl.semaphore_signal(barrier, inc=1, device_id=to, device_id_type=MESH)

    def greet_z(i, carry):
        greet(dev(x, y, (z + i) % nz, c))
        return carry

    lax.fori_loop(1, nz, greet_z, 0)
    for i in range(1, nx):
        greet(dev((x + i) % nx, y, z, c))
        greet(dev(x, (y + i) % ny, z, c))
    greet(dev(x, y, z, 1 - c))
    for i in range(nx):
        if i == 0:

            @pl.when(jnp.logical_not(on_diag))
            def _():
                greet(dev(x, x, z, c))

        else:
            greet(dev((x + i) % nx, x, z, c))
        greet(dev((x + i) % nx, x, z, 1 - c))

    for j in range(ny):
        kvst[j, 0] = sk[j * sub : (j + 1) * sub, :]
        kvst[j, 1] = sv[j * sub : (j + 1) * sub, :]
    for h in range(H):
        qst[h * TOK : (h + 1) * TOK, :] = sq[:, h * D : (h + 1) * D]
    gain = jnp.concatenate([sg[:, h * D : (h + 1) * D] for h in range(H)], axis=0)
    g0 = gain.astype(BF).astype(F32)
    g1 = (gain - g0).astype(BF).astype(F32)
    g2 = gain - g0 - g1
    qst[H * TOK :, :] = jnp.concatenate([g0, g1, g2, jnp.zeros_like(g0)], axis=0).astype(BF)
    for layer, ref in ((0, lw), (1, sw)):
        wide = ref[...].astype(F32)
        for j in range(ny):
            for k in range(2):
                at = (j * 2 + k) * NOUT
                wst[j, k, layer] = wide[:, at : at + NOUT]

    def rate_of(e):
        return jnp.exp2(-jnp.full((8, D), e, jnp.int32).astype(F32))[:1]

    for h in range(H):
        rate = rate_of(de[h])
        back = (TOK - 1 - iota((TOK, D), 0)).astype(F32)
        scaled = lk[:, h * D : (h + 1) * D].astype(F32) * jnp.exp(-rate * back)
        hi, lo_ = split2(scaled.T)
        v = lv[:, h * D : (h + 1) * D]
        update = (dot(hi, v) + dot(lo_, v)).astype(BF)
        per = D // part
        for k in range(per):
            us[h * per + k] = update[k * part : (k + 1) * part, :]

    n_greet = (nz - 1) + 2 * (nx - 1) + 1 + 2 * nx - jnp.where(on_diag, 1, 0)
    pl.semaphore_wait(barrier, n_greet)

    def plane_send(src, dst, ssem, rsem, i, other=False):
        j = (y + i) % ny
        to = dev(y, j, z, 1 - c if other else c)
        if i == 0 and not other:

            @pl.when(on_diag)
            def _():
                pltpu.make_async_copy(src, dst, rsem).start()

            @pl.when(jnp.logical_not(on_diag))
            def _():
                remote(src, dst, ssem, rsem, to).start()

        else:
            remote(src, dst, ssem, rsem, to).start()

    def plane_sent(src, ssem, i, other=False):
        if i == 0 and not other:

            @pl.when(jnp.logical_not(on_diag))
            def _():
                pltpu.make_async_copy(src, src, ssem).wait()

        else:
            pltpu.make_async_copy(src, src, ssem).wait()

    def landed(dst, rsem):
        pltpu.make_async_copy(dst, dst, rsem).wait()

    for i in range(ny):
        plane_send(kvst.at[(y + i) % ny], kvg.at[:, x, 0], kvt_s.at[i], kvt_r.at[x], i)

    def u_copy(i):
        to = (z + i) % nz
        return remote(us.at[to], uland.at[z], ua_s.at[i], ua_r.at[i], dev(x, y, to, c))

    def u_start(i, carry):
        u_copy(i).start()
        return carry

    lax.fori_loop(1, nz, u_start, 0)
    for i in range(ny):
        for k in range(2):
            other = k == 1
            plane_send(
                wst.at[(y + i) % ny, 1 - c if other else c],
                wland.at[c, x], wt_s.at[k, i], wt_r.at[k, x], i, other,
            )
    for i in range(ny):
        plane_send(qst, qh.at[x], qt_s.at[i], qt_r.at[x], i)
    uland[z] = us[z]

    def kv_steps(stream, way):
        return half if stream == way else half - 1

    def kv_copy(stream, way, s):
        if way == 0:
            src, dst, to = (0 if s == 1 else 2 * s - 3), 2 * s - 1, (z + 1) % nz
        else:
            src, dst, to = 2 * s - 2, min(2 * s, nz - 1), (z + nz - 1) % nz
        return remote(
            kvg.at[stream, :, src], kvg.at[stream, :, dst],
            kv_s.at[stream, way, s - 1], kv_r.at[stream, way, s - 1], dev(x, y, to, c),
        )

    def w_copy(stream, way, s):
        if way == 0:
            at, to = (z + nz - s + 1) % nz, (z + 1) % nz
        else:
            at, to = (z + s - 1) % nz, (z + nz - 1) % nz
        block = wg.at[stream, :, at]
        return remote(
            block, block, wr_s.at[stream, way, s - 1], wr_r.at[stream, way, s - 1], dev(x, y, to, c)
        )

    def ring(copy, s):
        for stream in range(2):
            for way in range(2):
                if s > 0 and s <= kv_steps(stream, way):
                    copy(stream, way, s).wait_recv()
                if s + 1 <= kv_steps(stream, way):
                    copy(stream, way, s + 1).start()

    for i in range(nx):
        landed(kvg.at[:, i, 0], kvt_r.at[i])
    ring(kv_copy, 0)
    for k in range(2):
        for i in range(nx):
            landed(wland.at[0, i], wt_r.at[k, i])
    for layer in range(2):
        for k in range(2):
            slab = jnp.concatenate([wland[k, i, layer] for i in range(nx)], axis=0)
            wg[layer, k, z] = slab.astype(BF)
    ring(w_copy, 0)

    def u_wait(i, carry):
        u_copy(i).wait_recv()
        return carry

    lax.fori_loop(1, nz, u_wait, 0)
    own = z * part // D
    lam = rate_of(de[own]) * float(TOK)
    step = jnp.exp(-lam)
    total = jnp.zeros((part, D), F32)
    before = []
    for i in range(nz):
        before.append(total)
        total = step * total + uland[i].astype(F32)
    tx[x] = total

    def tx_copy(i):
        return remote(tx.at[x], tx.at[x], tx_s.at[i], tx_r.at[i], dev((x + i) % nx, y, z, c))

    for i in range(1, nx):
        tx_copy(i).start()

    ring(kv_copy, 1)
    ring(w_copy, 1)

    for i in range(1, nx):
        tx_copy(i).wait_recv()
    xf = jnp.full((8, D), x, jnp.int32).astype(F32)[:1]
    first = pl.multiple_of((z * part) % D, part)
    entering = jnp.exp(-lam * nz * xf) * st[own, pl.ds(first, part), :]
    for i in range(nx):
        gap = xf - 1.0 - i
        weight = jnp.where(gap >= 0, jnp.exp(-lam * nz * jnp.maximum(gap, 0.0)), 0.0)
        entering += weight * tx[i]
    for i in range(nz):
        ss[i] = (before[i] + jnp.exp(-lam * float(i)) * entering).astype(BF)

    def s_copy(i):
        to = (z + i) % nz
        return remote(ss.at[to], sland.at[z], sa_s.at[i], sa_r.at[i], dev(x, y, to, c))

    def s_start(i, carry):
        s_copy(i).start()
        return carry

    lax.fori_loop(1, nz, s_start, 0)
    sland[z] = ss[z]

    ring(kv_copy, 2)
    ring(w_copy, 2)

    to_col = iota((depth, depth), 1)
    src_col = (to_col // rows) % nx * (nz * rows) + to_col // (nx * rows) * rows + to_col % rows
    perm[...] = jnp.where(iota((depth, depth), 0) == src_col, 1.0, 0.0).astype(BF)
    col = iota((TOK, span), 1)
    slot = col // sub
    far = (slot + 1) // 2
    least = jnp.where(slot % 2 == 1, far, nz - far)
    seen = (least <= z) | ((slot == 0) & (y * sub + col <= iota((TOK, span), 0)))
    bias[...] = jnp.where(seen, 0.0, NEG)

    def permuted(blocks):
        return dot(jnp.concatenate(blocks, axis=1).astype(BF), perm[...]).astype(BF)

    intra = []
    for h in range(H):
        cols = slice(h * D, (h + 1) * D)
        within = iota((TOK, TOK), 0) - iota((TOK, TOK), 1)
        rate = rate_of(de[h])
        inside = jnp.where(within >= 0, jnp.exp(-rate * jnp.maximum(within, 0).astype(F32)), 0.0)
        hi, lo_ = split2(dot_t(lq[:, cols], lk[:, cols]) * inside)
        intra.append(dot(hi, lv[:, cols]) + dot(lo_, lv[:, cols]))

    def s_wait(i, carry):
        s_copy(i).wait_recv()
        return carry

    lax.fori_loop(1, nz, s_wait, 0)
    ring(kv_copy, 3)
    ring(w_copy, 3)
    normed = []
    for h in range(H):
        cols = slice(h * D, (h + 1) * D)
        per = D // part
        state = jnp.concatenate([sland[h * per + k] for k in range(per)], axis=0)
        decay = jnp.exp(-rate_of(de[h]) * (iota((TOK, D), 0) + 1).astype(F32))
        normed.append(head_norm(intra[h] + dot(lq[:, cols], state) * decay, lg[:, cols]))
    ast = ag.at[2, 0, 0]
    ast[...] = permuted(normed)
    for i in range(ny):
        plane_send(ast, ag.at[0, c, x], lat_s.at[i], lat_r.at[x], i)

    for s in range(4, half + 1):
        ring(kv_copy, s)
        ring(w_copy, s)

    scale = 1.4426950408889634 / D**0.5
    for i in range(nx):
        landed(qh.at[i], qt_r.at[i])
    lane = iota((TOK, D), 1)
    packed = jnp.full((TOK, D), NEG, F32)
    for g in range(nx):

        def one_head(h, packed, g=g):
            at = pl.multiple_of(h * TOK, TOK)
            q = qh[g, pl.ds(at, TOK), :]
            scores = []
            for k in range(g + 1):
                raw = dot_t(q, kvg[0, k].reshape(span, D))
                scores.append(raw + bias[...] if k == g else raw)
            peak = jnp.full((TOK, 1), FLOOR, F32)
            for raw in scores:
                peak = jnp.maximum(peak, jnp.max(raw, axis=-1, keepdims=True))
            count = jnp.zeros((TOK, 1), F32)
            out = jnp.zeros((TOK, D), F32)
            for k, raw in enumerate(scores):
                weight = jnp.exp2((raw - peak) * scale)
                count += jnp.sum(weight, axis=-1, keepdims=True)
                out += dot(weight.astype(BF), kvg[1, k].reshape(span, D))
            some = count > 0
            safe = jnp.where(some, count, 1.0)
            osend[g, h] = (out / safe).astype(BF)
            lse = jnp.where(some, peak * scale + jnp.log2(safe), NEG)
            return jnp.where(lane == g * 8 + h, lse, packed)

        packed = lax.fori_loop(0, H, one_head, packed)
    turned = packed.T
    for g in range(nx):
        lsend[g] = turned[g * 8 : (g + 1) * 8, :]

    def o_copy(i):
        to = (y + i) % ny
        return remote(osend.at[to], oland.at[y], os_s.at[i], os_r.at[i], dev(x, to, z, c))

    def l_copy(i):
        to = (y + i) % ny
        return remote(lsend.at[to], lland.at[y], ls_s.at[i], ls_r.at[i], dev(x, to, z, c))

    for i in range(1, ny):
        l_copy(i).start()
        o_copy(i).start()
    oland[y] = osend[y]
    lland[y] = lsend[y]

    def forward(layer, block):
        ref = ag.at[layer, c, block]
        return remote(ref, ref, fw_s.at[layer, block], fw_r.at[layer, block], dev(x, y, z, 1 - c))

    for i in range(nx):
        landed(ag.at[0, 0, i], lat_r.at[i])
        forward(0, i).start()

    def c_copy(layer, i):
        to = (x + i) % nx
        return remote(
            csend.at[layer, to], cland.at[layer, x], cs_s.at[layer, i], cs_r.at[layer, i],
            dev(to, y, z, c),
        )

    def project(layer):
        w0 = wg[layer, 0].reshape(depth, NOUT)
        w1 = wg[layer, 1].reshape(depth, NOUT)
        for i in list(range(1, nx)) + [0]:
            block = (x + i) % nx
            forward(layer, block).wait_recv()
            partial = (dot(ag[layer, 0, block], w0) + dot(ag[layer, 1, block], w1)).astype(BF)
            if i == 0:
                cland[layer, x] = partial
            else:
                csend[layer, block] = partial
                c_copy(layer, i).start()

    project(0)

    for i in range(1, ny):
        l_copy(i).wait_recv()
        o_copy(i).wait_recv()
    lses = jnp.concatenate(
        [lland[j] for j in range(ny)] + [jnp.zeros((D - 8 * ny, D), F32)], axis=0
    ).T
    gains = qh[0, H * TOK :, :].astype(F32)
    gains = gains[0:4] + gains[4:8] + gains[8:12]
    normed = []
    for h in range(H):
        each = [lses[:, j * 8 + h : j * 8 + h + 1] for j in range(ny)]
        peak = functools.reduce(jnp.maximum, each)
        shares = [jnp.exp2(a - peak) for a in each]
        mixed = sum(w * oland[j, h].astype(F32) for j, w in enumerate(shares)) / sum(shares)
        normed.append(head_norm(mixed, gains[h : h + 1, :]))
    ag[1, c, y] = permuted(normed)

    def a_copy(i):
        ref = ag.at[1, c, y]
        return remote(ref, ref, sat_s.at[i], sat_r.at[i], dev(x, (y + i) % ny, z, c))

    for i in range(1, ny):
        a_copy(i).start()
    forward(1, y).start()
    for i in range(1, ny):
        a_copy(i).wait_recv()
        forward(1, (y + ny - i) % ny).start()
    project(1)

    for layer, out in ((0, lo), (1, so)):
        for i in range(1, nx):
            c_copy(layer, i).wait_recv()
        out[...] = sum(cland[layer, i].astype(F32) for i in range(nx)).astype(BF)

    for i in range(ny):
        plane_sent(kvst.at[0], kvt_s.at[i], i)
        plane_sent(wst.at[0, 0], wt_s.at[0, i], i)
        plane_sent(wst.at[0, 0], wt_s.at[1, i], i, True)
        plane_sent(qst, qt_s.at[i], i)
        plane_sent(ast, lat_s.at[i], i)

    def far_wait(i, carry):
        u_copy(i).wait_send()
        s_copy(i).wait_send()
        return carry

    lax.fori_loop(1, nz, far_wait, 0)
    for i in range(1, nx):
        tx_copy(i).wait_send()
        o_copy(i).wait_send()
        l_copy(i).wait_send()
        a_copy(i).wait_send()
        for layer in range(2):
            c_copy(layer, i).wait_send()
    for i in range(nx):
        for layer in range(2):
            forward(layer, i).wait_send()
    for stream in range(2):
        for way in range(2):
            for s in range(1, kv_steps(stream, way) + 1):
                kv_copy(stream, way, s).wait_send()
                w_copy(stream, way, s).wait_send()


def local(nx, nz, *args):
    rows = args[-1].shape[0]
    ny = nx
    half = nz // 2
    sub = TOK // ny
    depth = H * D
    part = depth // nz
    args = list(args)
    args[8] = args[8].reshape(1, depth)
    args[9] = args[9].reshape(1, depth)
    vmem = pl.BlockSpec(memory_space=pltpu.VMEM)
    specs = [vmem] * 12
    specs[4] = pl.BlockSpec(memory_space=pltpu.SMEM)
    dma = pltpu.SemaphoreType.DMA
    scratch = [
        pltpu.VMEM((ny, 2, sub, D), BF),
        pltpu.VMEM((2, nx, nz, sub, D), BF),
        pltpu.VMEM((H * TOK + 16, D), BF),
        pltpu.VMEM((nx, H * TOK + 16, D), BF),
        pltpu.VMEM((ny, 2, 2, rows, NOUT), F32),
        pltpu.VMEM((2, nx, 2, rows, NOUT), F32),
        pltpu.VMEM((2, 2, nz, nx * rows, NOUT), BF),
        pltpu.VMEM((nz, part, D), BF),
        pltpu.VMEM((nz, part, D), BF),
        pltpu.VMEM((nx, part, D), F32),
        pltpu.VMEM((nz, part, D), BF),
        pltpu.VMEM((nz, part, D), BF),
        pltpu.VMEM((nx, H, TOK, D), BF),
        pltpu.VMEM((ny, H, TOK, D), BF),
        pltpu.VMEM((nx, 8, D), F32),
        pltpu.VMEM((ny, 8, D), F32),
        pltpu.VMEM((3, 2, nx, TOK, depth), BF),
        pltpu.VMEM((2, nx, TOK, NOUT), BF),
        pltpu.VMEM((2, nx, TOK, NOUT), BF),
        pltpu.VMEM((depth, depth), BF),
        pltpu.VMEM((TOK, nz * sub), F32),
    ]
    sems = [
        (ny,), (nx,), (2, ny), (2, nx), (ny,), (nx,),
        (nz,), (nz,), (nx,), (nx,), (nz,), (nz,),
        (2, 2, half), (2, 2, half), (2, 2, half), (2, 2, half),
        (ny,), (ny,), (ny,), (ny,), (ny,), (nx,), (ny,), (ny,),
        (2, nx), (2, nx), (2, nx), (2, nx),
    ]
    out = jax.ShapeDtypeStruct((TOK, NOUT), BF)
    return pl.pallas_call(
        functools.partial(kernel, nx, nz),
        out_shape=(out, out),
        in_specs=specs,
        out_specs=(vmem, vmem),
        scratch_shapes=scratch + [dma(s) for s in sems],
        compiler_params=pltpu.CompilerParams(
            collective_id=0, has_side_effects=True, vmem_limit_bytes=48 * 1024 * 1024
        ),
        name="plane_attention",
    )(*args)


def solution(mesh):
    nx = mesh.shape["head"] // 2
    nz = mesh.shape["ctx"] // nx
    placed = (
        P("ctx", "head"),
        P("ctx", "head"),
        P("ctx", "head"),
        P("head", None, None),
        P("head"),
        P("ctx", "head"),
        P("ctx", "head"),
        P("ctx", "head"),
        P("head"),
        P("head"),
        P(("head", "ctx"), None),
        P(("head", "ctx"), None),
    )
    return jax.shard_map(
        functools.partial(local, nx, nz),
        mesh=mesh,
        in_specs=placed,
        out_specs=(P("ctx", "head"), P("ctx", "head")),
        check_vma=False,
    )
```

time: 857 us -> 129 us (0.15)
  waiting for transfers between devices: 672 us -> 0 us
  blocking collectives: 123 us -> 0 us
  Pallas kernels: 0 us -> 117 us
  matrix products: 22.2 us -> 0 us
  between operations: 15 us -> 0.67 us
    all_gather x5 -> x0, waiting for transfers between devices: 591 us -> none  [the longest x1 195 us: carried_in(): gathered = jax.tree.map(lambda a: lax.all_gather(a, axis), part)]
    unnamed x1 -> x0, blocking collectives: 123 us -> none
    pallas_call x0 -> x1, Pallas kernels: none -> 117 us  [local(): pl.pallas_call(functools.partial(kernel, nx, nz), out_shape=(out, out), i...]
    unnamed x9 -> x0, waiting for transfers between devices: 80.3 us -> none
    dot_general x8 -> x0, matrix products: 22.2 us -> none  [the longest x1 8.46 us: local(): jnp.einsum('tcgu,ucd->tcgd', weights.astype(jnp.bfloat16), piece_values,...]
  transfers between devices with their start and end apart: 7 -> 0, of which waited for: 7 -> 0; matrix products, arithmetic and copies ran while one was open for 4% -> 0% of each run, Pallas kernels for 0% -> 0%
where the time goes in v1:
time: 129 us; the launch traced here: 128 us
  Pallas kernels  117 us (91%)
  local copies, waits for them, and re-layouts  10.3 us (8%)
    pallas_call x1, Pallas kernels, local(): pl.pallas_call(functools.partial(kernel, nx, nz), out_shape=(out, out), i...  117 us
    unnamed x26, local copies, waits for them, and re-layouts  10.3 us

profile of v1, /device:TPU:1, one launch (start us, length us, event | category | flops | bytes accessed | tf_op | source)
XLA Modules:
  0.0 128.1 jit_solution(10153954584927403835)
XLA Ops:
  0.6 0.0 copy-start.9
  0.6 0.0 copy-start.11
  0.7 0.7 copy-done.9
  1.3 0.0 copy-done.11
  1.3 0.0 copy-start
  1.3 0.9 copy-done
  2.3 0.0 copy-start.1
  2.3 0.9 copy-done.1
  3.2 0.0 copy-start.2
  3.2 0.9 copy-done.2
  4.1 0.0 copy-start.3
  4.1 0.9 copy-done.3
  5.0 0.0 copy-start.4
  5.0 0.9 copy-done.4
  5.9 0.0 copy-start.5
  5.9 0.8 copy-done.5
  6.7 0.0 copy-start.6
  6.7 0.8 copy-done.6
  7.5 0.0 copy-start.7
  7.5 0.8 copy-done.7
  8.2 0.0 copy-start.8
  8.2 0.8 copy-done.8
  9.0 0.0 copy-start.10
  9.0 0.7 copy-done.10
  9.7 117.2 %plane_attention.1 = (bf16[128,384]{1,0:T(8,128)(2,1)S(1)}, bf16[128,384]{1,0:T(8,128)(2,1)S(1)}) custom-call(bf16[128,512]{1,0:T(8,128)(2,1)S(1)} %copy-done.1, bf16[128,512]{1,0:T(8,128)(2,1)S(1)} %copy-done.2, bf16[128,512]{1,0:T(8,128)(2,1)S(1)} %copy-done.3, f32[4,128,128]{2,1,0:T(8,128)S(1)} %copy-done, s32[4]{0:T(128)S(1)} %copy-done.11, ...), custom_call_target="tpu_custom_call" | custom-call | tf_op jit(solution)/shard_map/plane_attention/pallas_call | solution.py:508
  126.9 0.6 copy.16
  127.5 0.6 copy.17
Async XLA Ops:
  0.6 0.7 copy-start.9
  0.6 0.7 copy-start.11
  1.3 1.0 copy-start
  2.3 0.9 copy-start.1
  3.2 0.9 copy-start.2
  4.1 0.9 copy-start.3
  5.0 0.9 copy-start.4
  5.9 0.8 copy-start.5
  6.7 0.8 copy-start.6
  7.5 0.8 copy-start.7
  8.2 0.8 copy-start.8
  9.0 0.7 copy-start.10

commit v2 on v1

v2 whole, which is shorter than its diff:
```python
import functools

import jax
import jax.numpy as jnp
from jax import lax
from jax.experimental import pallas as pl
from jax.experimental.pallas import tpu as pltpu
from jax.sharding import PartitionSpec as P

D = 128
H = 4
TOK = 128
NOUT = 384
MESH = pl.DeviceIdType.MESH
BF = jnp.bfloat16
F32 = jnp.float32
PARTS = 2
NEG = -1e30
FLOOR = -1e29


def dot(a, b):
    return jnp.dot(a, b, preferred_element_type=F32)


def dot_t(a, b):
    return lax.dot_general(a, b, (((1,), (1,)), ((), ())), preferred_element_type=F32)


def split2(a):
    hi = a.astype(BF)
    return hi, (a - hi.astype(F32)).astype(BF)


def iota(shape, axis):
    return lax.broadcasted_iota(jnp.int32, shape, axis)


def head_norm(values, gain):
    scale = lax.rsqrt(jnp.mean(values * values, axis=-1, keepdims=True) + 1e-06)
    return values * scale * gain


def kernel(
    nx, nz, lq_h, lk_h, lv_h, st_h, de, sq_h, sk_h, sv_h, lg_h, sg_h, lw_h, sw_h, lo, so,
    lq, lk, lv, st, lg, sg, lw, sw, in_s, kvst, kvg, qh, before, within_out, peaks, counts, acc, wst, wland, wg, us, uland, tx, ss, sland,
    osend, oland, lsend, lland, ag, csend, cland, perm, bias,
    kvt_s, kvt_r, wt_s, wt_r, qt_s, qt_r, ua_s, ua_r, tx_s, tx_r, sa_s, sa_r,
    kv_s, kv_r, wr_s, wr_r, os_s, os_r, ls_s, ls_r, at_s, at_r,
    fw_s, fw_r, cs_s, cs_r,
):
    ny = nx
    half = nz // 2
    direct = 2 if nz > 4 else 1
    rows = lw_h.shape[0]
    sub = TOK // ny
    span = nz * sub
    depth = H * D
    part = depth // nz
    ctx, head = lax.axis_index("ctx"), lax.axis_index("head")
    x, z = ctx // nz, ctx % nz
    y, c = head // 2, head % 2

    def dev(dx, dy, dz, dc):
        return (dx * nz + dz, dy * 2 + dc)

    def remote(src, dst, ssem, rsem, to):
        return pltpu.make_async_remote_copy(
            src_ref=src, dst_ref=dst, send_sem=ssem, recv_sem=rsem, device_id=to, device_id_type=MESH
        )

    on_diag = x == y

    loads = {}

    def load(name, pairs):
        loads[name] = []
        for src, dst in pairs:
            sem = in_s.at[sum(len(v) for v in loads.values())]
            loads[name].append(pltpu.make_async_copy(src, dst, sem))
            loads[name][-1].start()

    def loaded(name):
        for copy in loads[name]:
            copy.wait()

    pieces = [pl.ds(j * sub, sub) for j in range(ny)]
    load("kv", [(r.at[p], kvst.at[j, k]) for k, r in enumerate((sk_h, sv_h)) for j, p in enumerate(pieces)])
    load("w", [(lw_h, lw), (sw_h, sw)])
    load("lkv", [(lk_h, lk), (lv_h, lv)])
    load("q", [(sq_h.at[:, pl.ds(h * D, D)], qh.at[x, h]) for h in range(H)])
    load("lq", [(lq_h, lq), (lg_h, lg), (sg_h, sg), (st_h, st)])

    barrier = pltpu.get_barrier_semaphore()

    def greet(to):
        pl.semaphore_signal(barrier, inc=1, device_id=to, device_id_type=MESH)

    def greet_z(i, carry):
        greet(dev(x, y, (z + i) % nz, c))
        return carry

    lax.fori_loop(1, nz, greet_z, 0)
    for i in range(nx):
        if i > 0:
            greet(dev((x + i) % nx, y, z, c))
        greet(dev((x + i) % nx, y, z, 1 - c))
        for d in range(1, direct + 1):
            if i > 0:
                greet(dev((x + i) % nx, y, (z + d) % nz, c))
                greet(dev((x + i) % nx, y, (z + nz - d) % nz, c))
    for i in range(ny):
        if i == 0:

            @pl.when(jnp.logical_not(on_diag))
            def _():
                greet(dev(y, y, z, c))

        else:
            greet(dev(y, (y + i) % ny, z, c))

    n_greet = (nz - 1) + 3 * nx - 1 - jnp.where(on_diag, 1, 0) + 2 * direct * (nx - 1)

    def rate_of(e):
        return jnp.exp2(-jnp.full((8, D), e, jnp.int32).astype(F32))[:1]

    def landed(dst, rsem):
        pltpu.make_async_copy(dst, dst, rsem).wait()

    loaded("w")
    for layer, ref in ((0, lw), (1, sw)):
        wide = ref[...].astype(F32)
        for j in range(nx):
            for k in range(2):
                at = (j * 2 + k) * NOUT
                wst[j, k, layer] = wide[:, at : at + NOUT]
    loaded("kv")
    loaded("q")
    loaded("lkv")
    pl.semaphore_wait(barrier, n_greet)

    reach = [0] + [d * e for d in range(1, direct + 1) for e in (1, -1)]

    def slot_of(d):
        return 0 if d == 0 else 2 * d - 1 if d > 0 else -2 * d

    def kvt_copy(n, i):
        to, d = (x + i) % nx, reach[n]
        return remote(
            kvst.at[to], kvg.at[:, x, slot_of(d)], kvt_s.at[n, i], kvt_r.at[n, i],
            dev(to, y, (z + nz + d) % nz, c),
        )

    def wt_copy(k, i):
        to, core = (x + i) % nx, 1 - c if k else c
        return remote(wst.at[to, core], wland.at[c, x], wt_s.at[k, i], wt_r.at[k, i], dev(to, y, z, core))

    def along_x(ref, ssem, rsem, i):
        return remote(ref, ref, ssem.at[i], rsem.at[i], dev((x + i) % nx, y, z, c))

    def q_copy(i):
        return along_x(qh.at[x], qt_s, qt_r, i)

    far_first = sorted(range(len(reach)), key=lambda n: -abs(reach[n]))
    for n in far_first:
        for i in range(nx):
            if i > 0 or reach[n] != 0:
                kvt_copy(n, i).start()
    kvg[:, x, 0] = kvst[x]

    for h in range(H):
        rate = rate_of(de[h])
        back = (TOK - 1 - iota((TOK, D), 0)).astype(F32)
        scaled = lk[:, h * D : (h + 1) * D].astype(F32) * jnp.exp(-rate * back)
        hi, lo_ = split2(scaled.T)
        v = lv[:, h * D : (h + 1) * D]
        update = (dot(hi, v) + dot(lo_, v)).astype(BF)
        per = D // part
        for k in range(per):
            us[h * per + k] = update[k * part : (k + 1) * part, :]

    def u_copy(i):
        to = (z + i) % nz
        return remote(us.at[to], uland.at[z], ua_s.at[i], ua_r.at[i], dev(x, y, to, c))

    def u_start(i, carry):
        u_copy(i).start()
        return carry

    lax.fori_loop(1, nz, u_start, 0)
    for i in range(nx):
        for k in range(2):
            if i + k > 0:
                wt_copy(k, i).start()
    wland[c, x] = wst[x, c]
    for i in range(1, nx):
        q_copy(i).start()
    uland[z] = us[z]

    def last_step(stream, way):
        return half if stream == way else half - 1

    def kv_copy(stream, way, s):
        if way == 0:
            src, dst, to = (0 if s == 1 else 2 * s - 3), 2 * s - 1, (z + 1) % nz
        else:
            src, dst, to = 2 * s - 2, min(2 * s, nz - 1), (z + nz - 1) % nz
        return remote(
            kvg.at[stream, :, src], kvg.at[stream, :, dst],
            kv_s.at[stream, way, s - 1], kv_r.at[stream, way, s - 1], dev(x, y, to, c),
        )

    def w_copy(stream, way, s):
        if way == 0:
            at, to = (z + nz - s + 1) % nz, (z + 1) % nz
        else:
            at, to = (z + s - 1) % nz, (z + nz - 1) % nz
        block = wg.at[stream, :, at]
        return remote(
            block, block, wr_s.at[stream, way, s - 1], wr_r.at[stream, way, s - 1], dev(x, y, to, c)
        )

    def ring(copy, s, begin=False):
        for stream in range(2):
            for way in range(2):
                if not begin and s <= last_step(stream, way):
                    copy(stream, way, s).wait_recv()
                if s + 1 <= last_step(stream, way):
                    copy(stream, way, s + 1).start()

    for n in far_first:
        for i in range(nx):
            if i > 0 or reach[n] != 0:
                kvt_copy(n, i).wait_recv()
        if n == 2 * direct:
            ring(kv_copy, direct, True)

    for i in range(nx):
        for k in range(2):
            if i + k > 0:
                wt_copy(k, i).wait_recv()
    for layer in range(2):
        for k in range(2):
            slab = jnp.concatenate([wland[k, i, layer] for i in range(nx)], axis=0)
            wg[layer, k, z] = slab.astype(BF)
    ring(w_copy, 0, True)

    to_col = iota((depth, depth), 1)
    src_col = (to_col // rows) % nx * (nz * rows) + to_col // (nx * rows) * rows + to_col % rows
    perm[...] = jnp.where(iota((depth, depth), 0) == src_col, 1.0, 0.0).astype(BF)
    col = iota((TOK, span), 1)
    slot = col // sub
    far = (slot + 1) // 2
    least = jnp.where(slot % 2 == 1, far, nz - far)
    seen = (least <= z) | ((slot == 0) & (x * sub + col <= iota((TOK, span), 0)))
    bias[...] = jnp.where(seen, 0.0, NEG)

    def permuted(blocks):
        return dot(jnp.concatenate(blocks, axis=1).astype(BF), perm[...]).astype(BF)

    loaded("lq")
    for h in range(H):
        cols = slice(h * D, (h + 1) * D)
        within = iota((TOK, TOK), 0) - iota((TOK, TOK), 1)
        rate = rate_of(de[h])
        inside = jnp.where(within >= 0, jnp.exp(-rate * jnp.maximum(within, 0).astype(F32)), 0.0)
        hi, lo_ = split2(dot_t(lq[:, cols], lk[:, cols]) * inside)
        within_out[h] = dot(hi, lv[:, cols]) + dot(lo_, lv[:, cols])

    def tx_copy(i):
        return along_x(tx.at[x], tx_s, tx_r, i)

    own = z * part // D
    lam = rate_of(de[own]) * float(TOK)

    def state_rows():
        def u_wait(i, carry):
            u_copy(i).wait_recv()
            return carry

        lax.fori_loop(1, nz, u_wait, 0)
        step = jnp.exp(-lam)
        total = jnp.zeros((part, D), F32)
        for i in range(nz):
            before[i] = total
            total = step * total + uland[i].astype(F32)
        tx[x] = total
        for i in range(1, nx):
            tx_copy(i).start()

    def s_copy(i):
        to = (z + i) % nz
        return remote(ss.at[to], sland.at[z], sa_s.at[i], sa_r.at[i], dev(x, y, to, c))

    def state_back():
        for i in range(1, nx):
            tx_copy(i).wait_recv()
        xf = jnp.full((8, D), x, jnp.int32).astype(F32)[:1]
        first = pl.multiple_of((z * part) % D, part)
        entering = jnp.exp(-lam * nz * xf) * st[own, pl.ds(first, part), :]
        for i in range(nx):
            gap = xf - 1.0 - i
            weight = jnp.where(gap >= 0, jnp.exp(-lam * nz * jnp.maximum(gap, 0.0)), 0.0)
            entering += weight * tx[i]
        for i in range(nz):
            ss[i] = (before[i] + jnp.exp(-lam * float(i)) * entering).astype(BF)

        def s_start(i, carry):
            s_copy(i).start()
            return carry

        lax.fori_loop(1, nz, s_start, 0)
        sland[z] = ss[z]

    some_tok = TOK // PARTS

    def tokens(p):
        return pl.ds(p * some_tok, some_tok)

    def a_copy(layer, i, p):
        return along_x(ag.at[layer, c, x, tokens(p)], at_s.at[layer, p], at_r.at[layer, p], i)

    def forward(layer, block, p):
        ref = ag.at[layer, c, block, tokens(p)]
        return remote(ref, ref, fw_s.at[layer, p, block], fw_r.at[layer, p, block], dev(x, y, z, 1 - c))

    def spread(layer, p):
        for i in range(1, nx):
            a_copy(layer, i, p).start()
        forward(layer, x, p).start()

    def passed_on(layer, p):
        for i in range(1, nx):
            a_copy(layer, i, p).wait_recv()
            forward(layer, (x + nx - i) % nx, p).start()

    def lightning_out():
        def s_wait(i, carry):
            s_copy(i).wait_recv()
            return carry

        lax.fori_loop(1, nz, s_wait, 0)
        normed = []
        for h in range(H):
            cols = slice(h * D, (h + 1) * D)
            per = D // part
            state = jnp.concatenate([sland[h * per + k] for k in range(per)], axis=0)
            decay = jnp.exp(-rate_of(de[h]) * (iota((TOK, D), 0) + 1).astype(F32))
            out = within_out[h] + dot(lq[:, cols], state) * decay
            normed.append(head_norm(out, lg[:, cols]))
        ag[0, c, x] = permuted(normed)
        for p in range(PARTS):
            spread(0, p)

    scale = 1.4426950408889634 / D**0.5
    lane = iota((TOK, D), 1)
    cut = nz - 4 if nz > 4 else 2
    bounds = (0, cut, nz)

    def o_copy(i, p):
        to = (x + i) % nx
        return remote(osend.at[to, p], oland.at[x, p], os_s.at[p, i], os_r.at[p, i], dev(to, y, z, c))

    def l_copy(i):
        to = (x + i) % nx
        return remote(lsend.at[to], lland.at[x], ls_s.at[i], ls_r.at[i], dev(to, y, z, c))

    def attend(g, chunk):
        keys = slice(bounds[chunk], bounds[chunk + 1])
        width = (bounds[chunk + 1] - bounds[chunk]) * sub
        cols = slice(bounds[chunk] * sub, bounds[chunk + 1] * sub)

        q = qh[g].reshape(depth, D)
        if chunk == 0:
            old = jnp.full((depth, 1), FLOOR, F32)
        else:
            old = peaks[g][:, :1]
        scores = []
        peak = old
        for k in range(g + 1):
            raw = dot_t(q, kvg[0, k, keys].reshape(width, D))
            if k == g:
                mask = bias[:, cols]
                raw = (raw.reshape(H, TOK, width) + mask[None]).reshape(depth, width)
            peak = jnp.maximum(peak, jnp.max(raw, axis=-1, keepdims=True))
            scores.append(raw)
        if chunk == 0:
            count = jnp.zeros((depth, 1), F32)
            out = jnp.zeros((depth, D), F32)
        else:
            fade = jnp.exp2((old - peak) * scale)
            count = counts[g][:, :1] * fade
            out = acc[g] * fade
        for k, raw in enumerate(scores):
            weight = jnp.exp2((raw - peak) * scale)
            count += jnp.sum(weight, axis=-1, keepdims=True)
            out += dot(weight.astype(BF), kvg[1, k, keys].reshape(width, D))
        if chunk == 0:
            peaks[g] = jnp.broadcast_to(peak, (depth, D))
            counts[g] = jnp.broadcast_to(count, (depth, D))
            acc[g] = out
            return
        some = count > 0
        safe = jnp.where(some, count, 1.0)
        out = (out / safe).astype(BF).reshape(H, TOK, D)
        for p in range(PARTS):
            osend[g, p] = out[:, p * some_tok : (p + 1) * some_tok]
        lse = jnp.where(some, peak * scale + jnp.log2(safe), NEG)
        packed = jnp.full((TOK, D), NEG, F32)
        for h in range(H):
            packed = jnp.where(lane == h, lse[h * TOK : (h + 1) * TOK], packed)
        lsend[g] = packed.T[:8, :]

    def outputs_out():
        for i in range(1, nx):
            l_copy(i).start()
        for p in range(PARTS):
            for i in range(1, nx):
                o_copy(i, p).start()
        oland[x] = osend[x]
        lland[x] = lsend[x]

    def c_copy(layer, i, p):
        to = (x + i) % nx
        return remote(
            csend.at[layer, to, tokens(p)], cland.at[layer, y, tokens(p)],
            cs_s.at[layer, p, i], cs_r.at[layer, p, y], dev(to, x, z, c),
        )

    def project(layer, parts):
        for p in parts:
            for i in range(nx):
                forward(layer, i, p).wait_recv()
        low, tall = parts[0] * some_tok, len(parts) * some_tok
        at = pl.ds(low, tall)
        partial = sum(
            dot(ag[layer, k, :, at].reshape(nx * tall, depth), wg[layer, k].reshape(depth, NOUT))
            for k in range(2)
        )
        csend[layer, :, at] = partial.astype(BF).reshape(nx, tall, NOUT)
        for p in parts:
            for i in range(1, nx):
                c_copy(layer, i, p).start()

            @pl.when(on_diag)
            def _(p=p):
                cland[layer, y, tokens(p)] = csend[layer, x, tokens(p)]

            @pl.when(jnp.logical_not(on_diag))
            def _(p=p):
                c_copy(layer, 0, p).start()

    def share_logs():
        for i in range(1, nx):
            l_copy(i).wait_recv()
        packed = [lland[j] for j in range(nx)] + [jnp.zeros((D - 8 * nx, D), F32)]
        return jnp.concatenate(packed, axis=0).T

    def combine(lses, p):
        for i in range(1, nx):
            o_copy(i, p).wait_recv()
        lses = lses[p * some_tok : (p + 1) * some_tok]
        normed = []
        for h in range(H):
            each = [lses[:, j * 8 + h : j * 8 + h + 1] for j in range(nx)]
            peak = functools.reduce(jnp.maximum, each)
            shares = [jnp.exp2(a - peak) for a in each]
            mixed = sum(w * oland[j, p, h].astype(F32) for j, w in enumerate(shares)) / sum(shares)
            normed.append(head_norm(mixed, sg[:, h * D : (h + 1) * D]))
        ag[1, c, x, tokens(p)] = permuted(normed)

    kv_next, w_next = [direct + 1], [1]

    def kv_step():
        if kv_next[0] <= half:
            ring(kv_copy, kv_next[0])
            kv_next[0] += 1

    def w_step():
        if w_next[0] <= half:
            ring(w_copy, w_next[0])
            w_next[0] += 1

    kv_step()
    w_step()
    kv_step()
    w_step()
    state_rows()
    kv_step()
    w_step()
    state_back()
    for i in range(1, nx):
        q_copy(i).wait_recv()
    kv_step()
    w_step()
    attend(nx - 1, 0)
    kv_step()
    w_step()
    for g in range(nx - 2, -1, -1):
        attend(g, 0)
    while kv_next[0] <= half:
        kv_step()
    lightning_out()
    for g in range(nx - 1, -1, -1):
        attend(g, 1)
    outputs_out()
    w_step()
    w_step()
    lses = share_logs()
    for p in range(PARTS):
        combine(lses, p)
        spread(1, p)
    while w_next[0] <= half:
        w_step()
    for p in range(PARTS):
        passed_on(0, p)
    project(0, range(PARTS))
    for p in range(PARTS):
        passed_on(1, p)
        project(1, [p])

    for layer, out in ((0, lo), (1, so)):
        for p in range(PARTS):
            for i in range(1, ny):
                src = (y + i) % ny
                landed(cland.at[layer, src, tokens(p)], cs_r.at[layer, p, src])

            @pl.when(jnp.logical_not(on_diag))
            def _(layer=layer, p=p):
                landed(cland.at[layer, y, tokens(p)], cs_r.at[layer, p, y])

        out[...] = sum(cland[layer, i].astype(F32) for i in range(ny)).astype(BF)

    for n in far_first:
        for i in range(nx):
            if i > 0 or reach[n] != 0:
                kvt_copy(n, i).wait_send()
    for i in range(nx):
        for k in range(2):
            if i + k > 0:
                wt_copy(k, i).wait_send()
    def far_wait(i, carry):
        u_copy(i).wait_send()
        s_copy(i).wait_send()
        return carry

    lax.fori_loop(1, nz, far_wait, 0)
    for i in range(1, nx):
        tx_copy(i).wait_send()
        q_copy(i).wait_send()
        l_copy(i).wait_send()
        for p in range(PARTS):
            o_copy(i, p).wait_send()
            for layer in range(2):
                a_copy(layer, i, p).wait_send()
                c_copy(layer, i, p).wait_send()

    @pl.when(jnp.logical_not(on_diag))
    def _():
        for layer in range(2):
            for p in range(PARTS):
                c_copy(layer, 0, p).wait_send()

    for i in range(nx):
        for layer in range(2):
            for p in range(PARTS):
                forward(layer, i, p).wait_send()
    for stream in range(2):
        for way in range(2):
            for s in range(1, last_step(stream, way) + 1):
                if s > direct:
                    kv_copy(stream, way, s).wait_send()
                w_copy(stream, way, s).wait_send()


def local(nx, nz, *args):
    rows = args[-1].shape[0]
    ny = nx
    half = nz // 2
    sub = TOK // ny
    depth = H * D
    part = depth // nz
    args = list(args)
    args[8] = args[8].reshape(1, depth)
    args[9] = args[9].reshape(1, depth)
    vmem = pl.BlockSpec(memory_space=pltpu.VMEM)
    specs = [pl.BlockSpec(memory_space=pltpu.HBM)] * 12
    specs[4] = pl.BlockSpec(memory_space=pltpu.SMEM)
    dma = pltpu.SemaphoreType.DMA
    scratch = [
        pltpu.VMEM((TOK, depth), BF),
        pltpu.VMEM((TOK, depth), BF),
        pltpu.VMEM((TOK, depth), BF),
        pltpu.VMEM((H, D, D), F32),
        pltpu.VMEM((1, depth), F32),
        pltpu.VMEM((1, depth), F32),
        pltpu.VMEM((rows, args[10].shape[1]), BF),
        pltpu.VMEM((rows, args[10].shape[1]), BF),
        dma((2 * ny + H + 8,)),
        pltpu.VMEM((ny, 2, sub, D), BF),
        pltpu.VMEM((2, nx, nz, sub, D), BF),
        pltpu.VMEM((nx, H, TOK, D), BF),
        pltpu.VMEM((nz, part, D), F32),
        pltpu.VMEM((H, TOK, D), F32),
        pltpu.VMEM((nx, depth, D), F32),
        pltpu.VMEM((nx, depth, D), F32),
        pltpu.VMEM((nx, depth, D), F32),
        pltpu.VMEM((ny, 2, 2, rows, NOUT), F32),
        pltpu.VMEM((2, nx, 2, rows, NOUT), F32),
        pltpu.VMEM((2, 2, nz, nx * rows, NOUT), BF),
        pltpu.VMEM((nz, part, D), BF),
        pltpu.VMEM((nz, part, D), BF),
        pltpu.VMEM((nx, part, D), F32),
        pltpu.VMEM((nz, part, D), BF),
        pltpu.VMEM((nz, part, D), BF),
        pltpu.VMEM((nx, PARTS, H, TOK // PARTS, D), BF),
        pltpu.VMEM((nx, PARTS, H, TOK // PARTS, D), BF),
        pltpu.VMEM((nx, 8, D), F32),
        pltpu.VMEM((ny, 8, D), F32),
        pltpu.VMEM((2, 2, nx, TOK, depth), BF),
        pltpu.VMEM((2, nx, TOK, NOUT), BF),
        pltpu.VMEM((2, nx, TOK, NOUT), BF),
        pltpu.VMEM((depth, depth), BF),
        pltpu.VMEM((TOK, nz * sub), F32),
    ]
    sems = [
        (5, nx), (5, nx), (2, nx), (2, nx), (nx,), (nx,),
        (nz,), (nz,), (nx,), (nx,), (nz,), (nz,),
        (2, 2, half), (2, 2, half), (2, 2, half), (2, 2, half),
        (PARTS, nx), (PARTS, nx), (nx,), (nx,), (2, PARTS, nx), (2, PARTS, nx),
        (2, PARTS, nx), (2, PARTS, nx), (2, PARTS, nx), (2, PARTS, nx),
    ]
    out = jax.ShapeDtypeStruct((TOK, NOUT), BF)
    return pl.pallas_call(
        functools.partial(kernel, nx, nz),
        out_shape=(out, out),
        in_specs=specs,
        out_specs=(vmem, vmem),
        scratch_shapes=scratch + [dma(s) for s in sems],
        compiler_params=pltpu.CompilerParams(
            collective_id=0, has_side_effects=True, vmem_limit_bytes=62 * 1024 * 1024
        ),
        name="plane_attention",
    )(*args)


def solution(mesh):
    nx = mesh.shape["head"] // 2
    nz = mesh.shape["ctx"] // nx
    placed = (
        P("ctx", "head"),
        P("ctx", "head"),
        P("ctx", "head"),
        P("head", None, None),
        P("head"),
        P("ctx", "head"),
        P("ctx", "head"),
        P("ctx", "head"),
        P("head"),
        P("head"),
        P(("head", "ctx"), None),
        P(("head", "ctx"), None),
    )
    return jax.shard_map(
        functools.partial(local, nx, nz),
        mesh=mesh,
        in_specs=placed,
        out_specs=(P("ctx", "head"), P("ctx", "head")),
        check_vma=False,
    )
```

time: 129 us -> 91.9 us (0.71)
  Pallas kernels: 117 us -> 88.4 us
  local copies, waits for them, and re-layouts: 10.3 us -> 2.22 us
    pallas_call x1, Pallas kernels: 117 us -> 88.4 us  [local(): pl.pallas_call(functools.partial(kernel, nx, nz), out_shape=(out, out), i...]
    unnamed x26 -> x4, local copies, waits for them, and re-layouts: 10.3 us -> 2.22 us
where the time goes in v2:
time: 91.9 us; the launch traced here: 91.3 us
  Pallas kernels  88.4 us (96%)
  local copies, waits for them, and re-layouts  2.22 us (2%)
    pallas_call x1, Pallas kernels, local(): pl.pallas_call(functools.partial(kernel, nx, nz), out_shape=(out, out), i...  88.4 us
    unnamed x4, local copies, waits for them, and re-layouts  2.22 us

profile of v2, /device:TPU:1, one launch (start us, length us, event | category | flops | bytes accessed | tf_op | source)
XLA Modules:
  0.0 91.3 jit_solution(3277535197733758070)
XLA Ops:
  0.6 88.4 %plane_attention.1 = (bf16[128,384]{1,0:T(8,128)(2,1)}, bf16[128,384]{1,0:T(8,128)(2,1)}) custom-call(bf16[128,512]{1,0:T(8,128)(2,1)} %lq_h.1, bf16[128,512]{1,0:T(8,128)(2,1)} %lk_h.1, bf16[128,512]{1,0:T(8,128)(2,1)} %lv_h.1, f32[4,128,128]{2,1,0:T(8,128)} %st_h.1, s32[4]{0:T(128)} %de.1, bf16[128,512]{1,0:T(8,128)(2,1)} %sq_h.1, bf16[128,128]{1,0:T(8,128)(2,1)} %sk_h.1, ...), custom_call_target="tpu_custom_call" | custom-call | tf_op jit(solution)/shard_map/plane_attention/pallas_call | solution.py:634
  89.1 0.0 copy-start
  89.1 1.6 %copy.16 = bf16[128,384]{1,0:T(8,128)(2,1)} copy(bf16[128,384]{1,0:T(8,128)(2,1)} %get-tuple-element.4) | data formatting | bytes 196608
  90.7 0.0 copy-done
  90.7 0.6 copy.17
Async XLA Ops:
  89.1 1.6 %copy-start = (bf16[128,384]{1,0:T(8,128)(2,1)S(1)}, bf16[128,384]{1,0:T(8,128)(2,1)}, u32[]{:S(2)}) copy-start(bf16[128,384]{1,0:T(8,128)(2,1)} %get-tuple-element.5) | copy-start | bytes 294916

commit v3 on v2

--- a/solution.py
+++ b/solution.py
@@ -137,37 +137,6 @@
     loaded("kv")
     loaded("q")
     loaded("lkv")
-    pl.semaphore_wait(barrier, n_greet)
-
-    reach = [0] + [d * e for d in range(1, direct + 1) for e in (1, -1)]
-
-    def slot_of(d):
-        return 0 if d == 0 else 2 * d - 1 if d > 0 else -2 * d
-
-    def kvt_copy(n, i):
-        to, d = (x + i) % nx, reach[n]
-        return remote(
-            kvst.at[to], kvg.at[:, x, slot_of(d)], kvt_s.at[n, i], kvt_r.at[n, i],
-            dev(to, y, (z + nz + d) % nz, c),
-        )
-
-    def wt_copy(k, i):
-        to, core = (x + i) % nx, 1 - c if k else c
-        return remote(wst.at[to, core], wland.at[c, x], wt_s.at[k, i], wt_r.at[k, i], dev(to, y, z, core))
-
-    def along_x(ref, ssem, rsem, i):
-        return remote(ref, ref, ssem.at[i], rsem.at[i], dev((x + i) % nx, y, z, c))
-
-    def q_copy(i):
-        return along_x(qh.at[x], qt_s, qt_r, i)
-
-    far_first = sorted(range(len(reach)), key=lambda n: -abs(reach[n]))
-    for n in far_first:
-        for i in range(nx):
-            if i > 0 or reach[n] != 0:
-                kvt_copy(n, i).start()
-    kvg[:, x, 0] = kvst[x]
-
     for h in range(H):
         rate = rate_of(de[h])
         back = (TOK - 1 - iota((TOK, D), 0)).astype(F32)
@@ -179,20 +148,73 @@
         for k in range(per):
             us[h * per + k] = update[k * part : (k + 1) * part, :]
 
-    def u_copy(i):
-        to = (z + i) % nz
-        return remote(us.at[to], uland.at[z], ua_s.at[i], ua_r.at[i], dev(x, y, to, c))
-
-    def u_start(i, carry):
-        u_copy(i).start()
-        return carry
-
-    lax.fori_loop(1, nz, u_start, 0)
+    to_col = iota((depth, depth), 1)
+    src_col = (to_col // rows) % nx * (nz * rows) + to_col // (nx * rows) * rows + to_col % rows
+    perm[...] = jnp.where(iota((depth, depth), 0) == src_col, 1.0, 0.0).astype(BF)
+    col = iota((TOK, span), 1)
+    slot = col // sub
+    far = (slot + 1) // 2
+    least = jnp.where(slot % 2 == 1, far, nz - far)
+    seen = (least <= z) | ((slot == 0) & (x * sub + col <= iota((TOK, span), 0)))
+    bias[...] = jnp.where(seen, 0.0, NEG)
+
+    def permuted(blocks):
+        return dot(jnp.concatenate(blocks, axis=1).astype(BF), perm[...]).astype(BF)
+
+    loaded("lq")
+    for h in range(H):
+        cols = slice(h * D, (h + 1) * D)
+        within = iota((TOK, TOK), 0) - iota((TOK, TOK), 1)
+        rate = rate_of(de[h])
+        inside = jnp.where(within >= 0, jnp.exp(-rate * jnp.maximum(within, 0).astype(F32)), 0.0)
+        hi, lo_ = split2(dot_t(lq[:, cols], lk[:, cols]) * inside)
+        within_out[h] = dot(hi, lv[:, cols]) + dot(lo_, lv[:, cols])
+
+    pl.semaphore_wait(barrier, n_greet)
+
+    reach = [0] + [d * e for d in range(1, direct + 1) for e in (1, -1)]
+
+    def slot_of(d):
+        return 0 if d == 0 else 2 * d - 1 if d > 0 else -2 * d
+
+    def kvt_copy(n, i):
+        to, d = (x + i) % nx, reach[n]
+        return remote(
+            kvst.at[to], kvg.at[:, x, slot_of(d)], kvt_s.at[n, i], kvt_r.at[n, i],
+            dev(to, y, (z + nz + d) % nz, c),
+        )
+
+    def wt_copy(k, i):
+        to, core = (x + i) % nx, 1 - c if k else c
+        return remote(wst.at[to, core], wland.at[c, x], wt_s.at[k, i], wt_r.at[k, i], dev(to, y, z, core))
+
+    def along_x(ref, ssem, rsem, i):
+        return remote(ref, ref, ssem.at[i], rsem.at[i], dev((x + i) % nx, y, z, c))
+
+    def q_copy(i):
+        return along_x(qh.at[x], qt_s, qt_r, i)
+
+    far_first = sorted(range(len(reach)), key=lambda n: -abs(reach[n]))
+    for n in far_first:
+        for i in range(nx):
+            if i > 0 or reach[n] != 0:
+                kvt_copy(n, i).start()
+    kvg[:, x, 0] = kvst[x]
+
     for i in range(nx):
         for k in range(2):
             if i + k > 0:
                 wt_copy(k, i).start()
     wland[c, x] = wst[x, c]
+    def u_copy(i):
+        to = (z + i) % nz
+        return remote(us.at[to], uland.at[z], ua_s.at[i], ua_r.at[i], dev(x, y, to, c))
+
+    def u_start(i, carry):
+        u_copy(i).start()
+        return carry
+
+    lax.fori_loop(1, nz, u_start, 0)
     for i in range(1, nx):
         q_copy(i).start()
     uland[z] = us[z]
@@ -244,28 +266,6 @@
             slab = jnp.concatenate([wland[k, i, layer] for i in range(nx)], axis=0)
             wg[layer, k, z] = slab.astype(BF)
     ring(w_copy, 0, True)
-
-    to_col = iota((depth, depth), 1)
-    src_col = (to_col // rows) % nx * (nz * rows) + to_col // (nx * rows) * rows + to_col % rows
-    perm[...] = jnp.where(iota((depth, depth), 0) == src_col, 1.0, 0.0).astype(BF)
-    col = iota((TOK, span), 1)
-    slot = col // sub
-    far = (slot + 1) // 2
-    least = jnp.where(slot % 2 == 1, far, nz - far)
-    seen = (least <= z) | ((slot == 0) & (x * sub + col <= iota((TOK, span), 0)))
-    bias[...] = jnp.where(seen, 0.0, NEG)
-
-    def permuted(blocks):
-        return dot(jnp.concatenate(blocks, axis=1).astype(BF), perm[...]).astype(BF)
-
-    loaded("lq")
-    for h in range(H):
-        cols = slice(h * D, (h + 1) * D)
-        within = iota((TOK, TOK), 0) - iota((TOK, TOK), 1)
-        rate = rate_of(de[h])
-        inside = jnp.where(within >= 0, jnp.exp(-rate * jnp.maximum(within, 0).astype(F32)), 0.0)
-        hi, lo_ = split2(dot_t(lq[:, cols], lk[:, cols]) * inside)
-        within_out[h] = dot(hi, lv[:, cols]) + dot(lo_, lv[:, cols])
 
     def tx_copy(i):
         return along_x(tx.at[x], tx_s, tx_r, i)
@@ -519,18 +519,6 @@
         passed_on(1, p)
         project(1, [p])
 
-    for layer, out in ((0, lo), (1, so)):
-        for p in range(PARTS):
-            for i in range(1, ny):
-                src = (y + i) % ny
-                landed(cland.at[layer, src, tokens(p)], cs_r.at[layer, p, src])
-
-            @pl.when(jnp.logical_not(on_diag))
-            def _(layer=layer, p=p):
-                landed(cland.at[layer, y, tokens(p)], cs_r.at[layer, p, y])
-
-        out[...] = sum(cland[layer, i].astype(F32) for i in range(ny)).astype(BF)
-
     for n in far_first:
         for i in range(nx):
             if i > 0 or reach[n] != 0:
@@ -553,13 +541,7 @@
             o_copy(i, p).wait_send()
             for layer in range(2):
                 a_copy(layer, i, p).wait_send()
-                c_copy(layer, i, p).wait_send()
-
-    @pl.when(jnp.logical_not(on_diag))
-    def _():
-        for layer in range(2):
-            for p in range(PARTS):
-                c_copy(layer, 0, p).wait_send()
+
 
     for i in range(nx):
         for layer in range(2):
@@ -571,6 +553,27 @@
                 if s > direct:
                     kv_copy(stream, way, s).wait_send()
                 w_copy(stream, way, s).wait_send()
+
+    for layer, out in ((0, lo), (1, so)):
+        for p in range(PARTS):
+            for i in range(1, ny):
+                src = (y + i) % ny
+                landed(cland.at[layer, src, tokens(p)], cs_r.at[layer, p, src])
+
+            @pl.when(jnp.logical_not(on_diag))
+            def _(layer=layer, p=p):
+                landed(cland.at[layer, y, tokens(p)], cs_r.at[layer, p, y])
+
+        out[...] = sum(cland[layer, i].astype(F32) for i in range(ny)).astype(BF)
+
+    for layer in range(2):
+        for p in range(PARTS):
+            for i in range(1, nx):
+                c_copy(layer, i, p).wait_send()
+
+            @pl.when(jnp.logical_not(on_diag))
+            def _(layer=layer, p=p):
+                c_copy(layer, 0, p).wait_send()
 
 
 def local(nx, nz, *args):
@@ -638,7 +641,7 @@
         out_specs=(vmem, vmem),
         scratch_shapes=scratch + [dma(s) for s in sems],
         compiler_params=pltpu.CompilerParams(
-            collective_id=0, has_side_effects=True, vmem_limit_bytes=62 * 1024 * 1024
+            collective_id=0, has_side_effects=True, vmem_limit_bytes=60 * 1024 * 1024
         ),
         name="plane_attention",
     )(*args)

time: 91.9 us -> 91.3 us (level)
  no operation moved by 1% of the time
where the time goes in v3:
time: 91.3 us; the launch traced here: 90.9 us
  Pallas kernels  88 us (96%)
  local copies, waits for them, and re-layouts  2.22 us (2%)
    pallas_call x1, Pallas kernels, local(): pl.pallas_call(functools.partial(kernel, nx, nz), out_shape=(out, out), i...  88 us
    unnamed x4, local copies, waits for them, and re-layouts  2.22 us

profile of v3, /device:TPU:1, one launch (start us, length us, event | category | flops | bytes accessed | tf_op | source)
XLA Modules:
  0.0 90.9 jit_solution(14777166311168994351)
XLA Ops:
  0.6 88.0 %plane_attention.1 = (bf16[128,384]{1,0:T(8,128)(2,1)}, bf16[128,384]{1,0:T(8,128)(2,1)}) custom-call(bf16[128,512]{1,0:T(8,128)(2,1)} %lq_h.1, bf16[128,512]{1,0:T(8,128)(2,1)} %lk_h.1, bf16[128,512]{1,0:T(8,128)(2,1)} %lv_h.1, f32[4,128,128]{2,1,0:T(8,128)} %st_h.1, s32[4]{0:T(128)} %de.1, bf16[128,512]{1,0:T(8,128)(2,1)} %sq_h.1, bf16[128,128]{1,0:T(8,128)(2,1)} %sk_h.1, ...), custom_call_target="tpu_custom_call" | custom-call | tf_op jit(solution)/shard_map/plane_attention/pallas_call | solution.py:637
  88.7 0.0 copy-start
  88.7 1.6 %copy.16 = bf16[128,384]{1,0:T(8,128)(2,1)} copy(bf16[128,384]{1,0:T(8,128)(2,1)} %get-tuple-element.4) | data formatting | bytes 196608
  90.3 0.0 copy-done
  90.3 0.6 copy.17
Async XLA Ops:
  88.7 1.6 %copy-start = (bf16[128,384]{1,0:T(8,128)(2,1)S(1)}, bf16[128,384]{1,0:T(8,128)(2,1)}, u32[]{:S(2)}) copy-start(bf16[128,384]{1,0:T(8,128)(2,1)} %get-tuple-element.5) | copy-start | bytes 294916
